TPU v7x, 512 devices: a whole 4x4x16 slice. The times are simulated.
512 devices in a mesh: dp: 128 (over x, z, core), tensor: 4 (over y).
Axes of the slice: x: 4, y: 4, z: 16, core: 2. Of those that a mesh axis runs over, the one named last changes fastest.
Arguments:
- grad: bfloat16 [48, 1441792], P(None, ('dp', 'tensor')), may hold values from -100 to 100
- momentum: float32 [48, 1441792], P(None, ('dp', 'tensor')), may hold values from -6 to 6
- owner: int32 [48], replicated, may hold values from 0 to 127, as said below
Outputs:
- new_momentum: float32 [48, 1441792], P(None, ('dp', 'tensor'))
- update: bfloat16 [48, 1441792], P(None, ('dp', 'tensor'))
- owned_rms: float32 [128, 2], P('dp')
Inputs may be any that keep to these rules, and one draw needn't show every extreme that they name: `owner`: each matrix's owning dp index; no index owns more than 2 matrices, and some index owns exactly 2.
All inputs are finite; a program needn't handle non-finite values.
Results may differ from a plain program's by a relative error of at most 0.012.
Values may be sent and summed in bfloat16 or wider, within the bound.
A program may use at most 64 MiB of HBM per device.

v0:
```python
import math

import jax
import jax.numpy as jnp
from jax import lax
from jax.sharding import PartitionSpec as P

HW = 704
ITERS = 2


beta_decay = 0.95
coef_a = 3.4445
coef_b = -4.775
coef_c = 2.0315
epsilon = 1e-07


def group_gram(iterate):
    partial_value = jnp.einsum("crh,crk->chk", iterate, iterate, preferred_element_type=jnp.float32)
    return lax.psum(partial_value.astype(jnp.bfloat16), "tensor").astype(jnp.float32)


def orthogonalize(owned_rows, total_rows):
    full_cols = owned_rows.shape[2]
    first = group_gram(owned_rows)
    squares = jnp.trace(first, axis1=1, axis2=2)
    inverse = 1.0 / (jnp.sqrt(squares) + epsilon)
    scale_out = math.sqrt(max(total_rows, full_cols))
    current = (first * (inverse * inverse)[:, None, None]).astype(jnp.bfloat16)
    iterate = owned_rows
    for iteration in range(ITERS):
        if iteration > 0:
            current = group_gram(iterate).astype(jnp.bfloat16)
        square = jnp.einsum("chk,ckj->chj", current, current, preferred_element_type=jnp.float32)
        poly = (coef_b * current.astype(jnp.float32) + coef_c * square).astype(jnp.bfloat16)
        product = jnp.einsum("crh,chk->crk", iterate, poly, preferred_element_type=jnp.float32)
        mixed = coef_a * iterate.astype(jnp.float32) + product
        if iteration == 0:
            mixed = mixed * inverse[:, None, None]
        if iteration == ITERS - 1:
            mixed = mixed * scale_out
        iterate = mixed.astype(jnp.bfloat16)
    return (iterate, jnp.sqrt(squares / (total_rows * full_cols)))


def on_device(grad, momentum, owner):
    matrices = grad.shape[0]
    flat_len = grad.shape[1]
    dp_count = lax.axis_size("dp")
    tp_count = lax.axis_size("tensor")
    sub_rows = flat_len // HW
    total_rows = sub_rows * tp_count * dp_count
    new_momentum = beta_decay * momentum + grad.astype(jnp.float32)
    nesterov = (grad.astype(jnp.float32) + beta_decay * new_momentum).astype(jnp.bfloat16)
    per_owner = (matrices + dp_count - 1) // dp_count
    capacity = per_owner + 1
    index = jnp.arange(matrices, dtype=jnp.int32)
    same_owner = owner[:, None] == owner[None, :]
    owner_rank = jnp.sum((same_owner & (index[:, None] < index[None, :])).astype(jnp.int32), axis=0)
    owner_ids = jnp.arange(dp_count, dtype=jnp.int32)
    owner_slots = jnp.arange(capacity, dtype=jnp.int32)
    owner_select = (
        (owner_rank[None, None, :] == owner_slots[:, None, None])
        & (owner[None, None, :] == owner_ids[None, :, None])
    ).astype(jnp.float32)
    selector_low = owner_select.astype(jnp.bfloat16)
    outgoing = jnp.einsum(
        "som,mq->soq", selector_low, nesterov, preferred_element_type=jnp.float32
    ).astype(jnp.bfloat16)
    arrived = lax.all_to_all(outgoing, "dp", split_axis=1, concat_axis=1, tiled=True)
    owned_rows = arrived.reshape(capacity, dp_count * sub_rows, HW)
    finished, slot_rms = orthogonalize(owned_rows, total_rows)
    leaving = finished.reshape(capacity, dp_count, sub_rows * HW)
    returned = lax.all_to_all(leaving, "dp", split_axis=1, concat_axis=1, tiled=True)
    update = jnp.einsum(
        "som,soq->mq", selector_low, returned, preferred_element_type=jnp.float32
    ).astype(jnp.bfloat16)
    return (new_momentum, update, slot_rms.reshape(1, capacity))


def solution(mesh):
    return jax.shard_map(
        on_device,
        mesh=mesh,
        in_specs=(P(None, ("dp", "tensor")), P(None, ("dp", "tensor")), P()),
        out_specs=(P(None, ("dp", "tensor")), P(None, ("dp", "tensor")), P("dp", None)),
        check_vma=False,
    )
```

profile of v0, /device:TPU:1, one launch (start us, length us, event | category | flops | bytes accessed | tf_op | source)
XLA Modules:
  0.0 373.5 jit_solution(14944274168340644000)
XLA Ops:
  7.2 0.0 all-reduce.3.cloned.1.call-start
  7.2 0.7 iota_compare_fusion.1
  7.9 0.8 convert_reduce_fusion
  8.8 1.2 convert_add_fusion.1
  10.0 0.0 copy-done.1
  10.0 0.0 copy-start
  10.0 1.8 convolution_convert_fusion
  11.8 1.5 copy.30
  13.3 0.0 copy-done
  13.3 91.1 %all_to_all.10 = bf16[2,128,2816]{2,0,1:T(2,128)(2,1)S(1)} all-to-all(bf16[2,128,2816]{2,0,1:T(2,128)(2,1)S(1)} %copy.30), channel_id=1, replica_groups=mesh['dp'=128,'tensor'=4] {'dp'}, dimensions={1} | all-to-all | bytes 2883584 | tf_op jit(solution)/shard_map/all_to_all | solution.py:71
  104.4 0.1 copy.31
  104.6 1.8 reshape.82
  106.3 2.7 convolution_convert_fusion.2
  109.0 0.0 all-reduce.3.cloned.1.call-update
  109.0 0.2 all-reduce.5.cloned.1.call-start
  109.3 0.2 iota_compare_fusion
  109.4 0.7 copy.32
  110.1 68.0 %all-reduce.3.cloned.1.call-done = bf16[2,704,704]{2,1,0:T(8,128)(2,1)} async-done(((bf16[2,704,704]{2,1,0:T(8,128)(2,1)}), bf16[2,704,704]{2,1,0:T(8,128)(2,1)}) %all-reduce.3.cloned.1.call-update) | async-done | bytes 1982480 | tf_op jit(solution)/shard_map/psum | solution.py:21
  178.1 2.5 fusion
  180.6 0.5 fusion.22
  181.2 7.3 %multiply_convert_fusion.1 = bf16[2,512,704]{1,2,0:T(8,128)(2,1)} fusion(bf16[2,512,704]{1,2,0:T(8,128)(2,1)S(1)} %copy.32, bf16[2,512,704]{2,1,0:T(8,128)(2,1)S(1)} %reshape.82, f32[2]{0:T(128)S(1)} %get-tuple-element.4, bf16[2,704,704]{2,1,0:T(8,128)(2,1)} %all-reduce.3.cloned.1.call-done, f32[2]{0:T(128)S(1)} %get-tuple-element.3), kind=kOutput, calls=%fused_computation.10 | convolution fusion | flops 2425184256 | bytes 6307856 | tf_op jit(solution)/shard_map/crh,chk->crk/dot_general | solution.py:37
  188.5 4.5 %convolution_convert_fusion.1 = bf16[2,704,704]{2,1,0:T(8,128)(2,1)} fusion(bf16[2,512,704]{1,2,0:T(8,128)(2,1)} %multiply_convert_fusion.1), kind=kOutput, calls=%fused_computation.13 | convolution fusion | flops 1016012800 | bytes 3424256 | tf_op jit(solution)/shard_map/crh,crk->chk/dot_general | solution.py:20
  192.9 0.0 all-reduce.5.cloned.1.call-update
  193.0 75.2 %all-reduce.5.cloned.1.call-done = bf16[2,704,704]{2,1,0:T(8,128)(2,1)} async-done(((bf16[2,704,704]{2,1,0:T(8,128)(2,1)}), bf16[2,704,704]{2,1,0:T(8,128)(2,1)}) %all-reduce.5.cloned.1.call-update) | async-done | bytes 1982480 | tf_op jit(solution)/shard_map/psum | solution.py:21
  268.2 0.0 copy-done.5
  268.2 6.1 %multiply_convert_fusion = bf16[2,512,704]{1,2,0:T(8,128)(2,1)S(1)} fusion(bf16[2,512,704]{1,2,0:T(8,128)(2,1)S(1)} %copy-done.5, bf16[2,704,704]{2,1,0:T(8,128)(2,1)} %all-reduce.5.cloned.1.call-done), kind=kOutput, calls=%fused_computation.9 | convolution fusion | flops 2419236864 | bytes 4866048 | tf_op jit(solution)/shard_map/crh,chk->crk/dot_general | solution.py:37
  274.3 0.7 copy.38
  275.0 1.7 reshape.83
  276.7 1.5 copy.39
  278.2 0.0 copy-start.2
  278.2 87.3 %all_to_all.11 = bf16[2,128,2816]{2,0,1:T(2,128)(2,1)S(1)} all-to-all(bf16[2,128,2816]{2,0,1:T(2,128)(2,1)S(1)} %copy.39), channel_id=1, replica_groups=mesh['dp'=128,'tensor'=4] {'dp'}, dimensions={1} | all-to-all | bytes 2883584 | tf_op jit(solution)/shard_map/all_to_all | solution.py:75
  365.5 1.1 fusion.2
  (8 shorter events, 0.0 us)
Async XLA Ops:
  7.2 170.9 %all-reduce.3.cloned.1.call-start = ((), (), s32[]{:S(2)}) async-start(), calls=%async_computation.2 | async-start | bytes 4325376 | tf_op jit(solution)/shard_map/psum | solution.py:21
  7.9 2.0 copy-start.1
  8.8 1.2 copy-start.3
  10.0 3.3 copy-start
  109.0 159.2 %all-reduce.5.cloned.1.call-start = ((), (), s32[]{:S(2)}) async-start(), calls=%async_computation.3 | async-start | bytes 4325376 | tf_op jit(solution)/shard_map/psum | solution.py:21
  192.9 75.3 %copy-start.5 = (bf16[2,512,704]{1,2,0:T(8,128)(2,1)S(1)}, bf16[2,512,704]{1,2,0:T(8,128)(2,1)}, u32[]{:S(2)}) copy-start(bf16[2,512,704]{1,2,0:T(8,128)(2,1)} %multiply_convert_fusion.1) | copy-start | bytes 4325380
  278.2 87.3 %copy-start.2 = (pred[128,48]{0,1:T(8,128)(4,1)S(1)}, pred[128,48]{0,1:T(8,128)(4,1)}, u32[]{:S(2)}) copy-start(pred[128,48]{0,1:T(8,128)(4,1)} %copy-done.1) | copy-start | bytes 18436
  278.2 87.3 %copy-start.4 = (pred[2,48]{1,0:T(4,128)(4,1)S(1)}, pred[2,48]{1,0:T(4,128)(4,1)}, u32[]{:S(2)}) copy-start(pred[2,48]{1,0:T(4,128)(4,1)} %copy-done.3) | copy-start | bytes 292
Sparse Core Ops, SparseCore 0:
  109.1 68.9 all-reduce.2
  193.1 75.0 all-reduce.4
where the time goes:
time: 374 us; the launch traced here: 373 us
  blocking collectives  178 us (48%)
  waiting for transfers between devices  143 us (38%)
  matrix products  23.4 us (6%)
  between operations  14.2 us (4%)
  local copies, waits for them, and re-layouts  7.94 us (2%)
  other arithmetic  5.97 us (2%)
    psum x2, waiting for transfers between devices, group_gram(): lax.psum(partial_value.astype(jnp.bfloat16), 'tensor').astype(jnp.float32)  143 us
    all_to_all x1, blocking collectives, on_device(): lax.all_to_all(outgoing, 'dp', split_axis=1, concat_axis=1, tiled=True)  91.1 us
    all_to_all x1, blocking collectives, on_device(): lax.all_to_all(leaving, 'dp', split_axis=1, concat_axis=1, tiled=True)  87.3 us
    dot_general x2, matrix products, orthogonalize(): jnp.einsum('crh,chk->crk', iterate, poly, preferred_element_type=jnp.floa...  13.4 us
  transfers between devices with their start and end apart: 2, of which 2 were waited for; matrix products, arithmetic and copies ran while one was open for 0% of the time, Pallas kernels for 0%

commit v1 on v0

v1 whole, which is shorter than its diff:
```python
import math

import jax
import jax.numpy as jnp
from jax import lax
from jax.experimental import pallas as pl
from jax.experimental.pallas import tpu as pltpu
from jax.sharding import PartitionSpec as P

HW = 704
WIDE = 768
D = 2048
MATS = 48
CAP = 2
N_DP = 128
N_TENSOR = 4
SUB = 4
PLANE = N_DP // 2
PER_Y = MATS // N_TENSOR
BAND = SUB * N_TENSOR
ROWS = PLANE * BAND
TILE = 256

beta_decay = 0.95
coef_a = 3.4445
coef_b = -4.775
coef_c = 2.0315
epsilon = 1e-07

MESH = pl.DeviceIdType.MESH
f32, bf16 = jnp.float32, jnp.bfloat16


def home(j):
    return (j % 4) * 16 + (j * 4) // 3


def around(i):
    return (i + 1) // 2 if i % 2 else -(i // 2)


def one_hot(size, source):
    out_row = lax.broadcasted_iota(jnp.int32, (size, size), 0)
    in_row = lax.broadcasted_iota(jnp.int32, (size, size), 1)
    return (in_row == source(out_row)).astype(f32).astype(bf16)


def permuted(matrix, value):
    return jnp.dot(matrix, value, preferred_element_type=f32).astype(bf16)


def kernel(
    grad_ref, momentum_ref, owner_ref, momentum_out, update_out, rms_out,
    staged, from_y, bands, rows, turned, mid, done, total, half, other, gram, poly, back, to_y, land,
    send_y, recv_y, send_p, recv_p, send_g, recv_g, send_b, recv_b, send_z, recv_z, local_y, local_z,
):
    dp, y = lax.axis_index("dp"), lax.axis_index("tensor")
    core, place = dp % 2, dp // 2
    x, z = place // 16, place % 16
    mine = (3 * z + 3) // 4
    works = ((mine * 4) // 3 == z) & (mine % 4 == x) & (mine < PER_Y)
    bands_per = TILE // BAND

    barrier = pltpu.get_barrier_semaphore()
    for step in range(1, N_TENSOR):
        pl.semaphore_signal(barrier, inc=1, device_id=(dp, (y + step) % N_TENSOR), device_id_type=MESH)

    @pl.when(works)
    def _():
        pl.semaphore_signal(barrier, inc=1, device_id=(dp + 1 - 2 * core, y), device_id_type=MESH)

        def greet(step, carry):
            peer = (place + step) % PLANE
            pl.semaphore_signal(barrier, inc=1, device_id=(peer * 2 + core, y), device_id_type=MESH)
            return carry

        lax.fori_loop(1, PLANE, greet, 0)

    @pl.when(jnp.logical_not(works))
    def _():
        for j in range(PER_Y):
            pl.semaphore_signal(barrier, inc=1, device_id=(home(j) * 2 + core, y), device_id_type=MESH)

    grad = grad_ref[...].astype(f32)
    new_momentum = beta_decay * momentum_ref[...] + grad
    momentum_out[...] = new_momentum
    nesterov = (grad + beta_decay * new_momentum).astype(bf16)
    edge = jnp.zeros((MATS, WIDE - HW), bf16)
    by_row = jnp.concatenate(
        [jnp.concatenate([nesterov[:, HW * r:HW * (r + 1)], edge], axis=1) for r in range(SUB)], axis=0
    )
    to_matrix = one_hot(MATS * SUB, lambda o: (o % SUB) * MATS + o // SUB)
    staged[...] = permuted(to_matrix, by_row).reshape(N_TENSOR, PER_Y * SUB, WIDE)

    @pl.when(works)
    def _():
        pl.semaphore_wait(barrier, N_TENSOR - 1 + 1 + PLANE - 1)

    @pl.when(jnp.logical_not(works))
    def _():
        pl.semaphore_wait(barrier, N_TENSOR - 1 + PER_Y)

    def tile_at(i):
        t = (jnp.minimum(mine // 4, 2) + i) % 3
        return t, pl.ds(pl.multiple_of(t * BAND, BAND), BAND)

    def y_copy(src, dst, step, i, sends, recvs):
        peer = (y + step) % N_TENSOR
        at = tile_at(i)[1]
        return pltpu.make_async_remote_copy(
            src_ref=src.at[peer, at], dst_ref=dst.at[y, at],
            send_sem=sends.at[step - 1, i], recv_sem=recvs.at[step - 1, i],
            device_id=(dp, peer), device_id_type=MESH,
        )

    own = pltpu.make_async_copy(staged.at[y], from_y.at[y], local_y)
    own.start()
    for i in range(3):
        for step in range(1, N_TENSOR):
            y_copy(staged, from_y, step, i, send_y, recv_y).start()
    own.wait()

    def band_copy(i, k):
        j = tile_at(i)[0] * 4 + k
        return pltpu.make_async_remote_copy(
            src_ref=bands.at[j], dst_ref=rows.at[place], send_sem=send_p.at[i, k], recv_sem=recv_p.at[x],
            device_id=(home(j) * 2 + core, y), device_id_type=MESH,
        )

    def stays(i, k):
        return works & (tile_at(i)[0] * 4 + k == mine)

    regroup = one_hot(4 * BAND, lambda o: (o // SUB % 4) * BAND + (o // BAND) * SUB + o % SUB)
    for i in range(3):
        for step in range(1, N_TENSOR):
            y_copy(staged, from_y, step, i, send_y, recv_y).wait_recv()
        t, at = tile_at(i)
        tile = from_y[:, at, :].reshape(4 * BAND, WIDE)
        bands[pl.ds(4 * t, 4)] = permuted(regroup, tile).reshape(4, BAND, WIDE)
        for k in range(4):
            @pl.when(jnp.logical_not(stays(i, k)))
            def _():
                band_copy(i, k).start()

    @pl.when(works)
    def _():
        pltpu.make_async_copy(bands.at[mine], rows.at[place], recv_p.at[x]).start()

        def turn(ref, b):
            at = pl.multiple_of(b * TILE, TILE)
            turned[:, pl.ds(at, TILE)] = ref[pl.ds(b * bands_per, bands_per)].reshape(TILE, WIDE).T

        def swap(slot, c):
            return pltpu.make_async_remote_copy(
                src_ref=half.at[slot, c], dst_ref=other.at[slot, c], send_sem=send_g.at[slot, c], recv_sem=recv_g.at[slot, c],
                device_id=(dp + 1 - 2 * core, y), device_id_type=MESH,
            )

        def gram_sum(ref, slot):
            for c in range(WIDE // TILE):
                right = ref[:, :, c * TILE:(c + 1) * TILE].reshape(ROWS, TILE)
                half[slot, c] = jnp.dot(turned[...], right, preferred_element_type=f32).astype(bf16)
                swap(slot, c).start()
            for c in range(WIDE // TILE):
                swap(slot, c).wait()
                total[:, c * TILE:(c + 1) * TILE] = half[slot, c].astype(f32) + other[slot, c].astype(f32)

        def polynomial():
            current = gram[...]
            square = jnp.dot(current, current, preferred_element_type=f32)
            poly[...] = (coef_b * current.astype(f32) + coef_c * square).astype(bf16)

        def arrive(i, carry):
            b = (x + i) % 4
            column = rows.at[pl.ds(b * bands_per, bands_per)]
            pltpu.make_async_copy(column, column, recv_p.at[b]).wait()
            turn(rows, b)
            return carry

        lax.fori_loop(0, ROWS // TILE, arrive, 0)
        gram_sum(rows, 0)
        diagonal = lax.broadcasted_iota(jnp.int32, (TILE, TILE), 0) == lax.broadcasted_iota(jnp.int32, (TILE, TILE), 1)
        on_diagonal = sum(
            jnp.where(diagonal, total[c * TILE:(c + 1) * TILE, c * TILE:(c + 1) * TILE], 0.0) for c in range(WIDE // TILE)
        )
        squares = jnp.sum(jnp.sum(on_diagonal, axis=1, keepdims=True), axis=0, keepdims=True)
        inverse = 1.0 / (jnp.sqrt(squares) + epsilon)
        gram[...] = (total[...] * inverse * inverse).astype(bf16)
        polynomial()

        current = rows[...].reshape(ROWS, WIDE)
        product = jnp.dot(current, poly[...], preferred_element_type=f32)
        mixed = (coef_a * current.astype(f32) + product) * inverse
        mid[...] = mixed.astype(bf16).reshape(PLANE, BAND, WIDE)

        def turn_mid(b, carry):
            turn(mid, b)
            return carry

        lax.fori_loop(0, ROWS // TILE, turn_mid, 0)
        gram_sum(mid, 1)
        gram[...] = total[...].astype(bf16)
        polynomial()

        rms = jnp.sqrt(squares / (D * HW))
        high = rms.astype(bf16).astype(f32)
        low = rms - high
        lane = lax.broadcasted_iota(jnp.int32, (2 * TILE, WIDE), 1)

        def give(peer):
            return pltpu.make_async_remote_copy(
                src_ref=done.at[peer], dst_ref=back.at[mine], send_sem=send_b, recv_sem=recv_b.at[mine // 4],
                device_id=(peer * 2 + core, y), device_id_type=MESH,
            )

        def finish(i, carry):
            pair = (x // 2 + 1 + i) % 2
            at = pl.ds(pair * 2 * bands_per, 2 * bands_per)
            current = mid[at].reshape(2 * TILE, WIDE)
            product = jnp.dot(current, poly[...], preferred_element_type=f32)
            mixed = (coef_a * current.astype(f32) + product) * math.sqrt(max(D, HW))
            mixed = jnp.where(lane == HW, high, jnp.where(lane == HW + 1, low, mixed))
            done[at] = mixed.astype(bf16).reshape(2 * bands_per, BAND, WIDE)
            for k in range(16):
                for h in range(2):
                    peer = (pair * 2 + h) * 16 + (z + 16 + around(k)) % 16
                    if k:
                        give(peer).start()
                    else:
                        @pl.when(peer != place)
                        def _():
                            give(peer).start()
            return carry

        lax.fori_loop(0, 2, finish, 0)
        pltpu.make_async_copy(done.at[place], back.at[mine], recv_b.at[mine // 4]).start()

    for i in range(3):
        t, at = tile_at(i)
        four = back.at[pl.ds(4 * t, 4)]
        pltpu.make_async_copy(four, four, recv_b.at[t]).wait()
        tile = back[pl.ds(4 * t, 4)].reshape(4 * BAND, WIDE)
        to_y[:, at, :] = permuted(regroup, tile).reshape(4, BAND, WIDE)
        for step in range(1, N_TENSOR):
            y_copy(to_y, land, step, i, send_z, recv_z).start()

    own = pltpu.make_async_copy(to_y.at[y], land.at[y], local_z)
    own.start()

    index_m = lax.broadcasted_iota(jnp.int32, (MATS, MATS), 0)
    index_n = lax.broadcasted_iota(jnp.int32, (MATS, MATS), 1)
    owners = owner_ref[...].astype(f32)
    owner = jnp.sum(jnp.where(index_m == index_n, owners, 0.0), axis=1, keepdims=True)
    rank = jnp.sum(jnp.where((owner == owners) & (index_n < index_m), 1.0, 0.0), axis=1, keepdims=True)
    owned = owner == dp.astype(f32)

    @pl.when(works)
    def _():
        pltpu.make_async_copy(done.at[pl.ds(0, PLANE - 1)], done.at[pl.ds(0, PLANE - 1)], send_b).wait()

    for i in range(3):
        for k in range(4):
            @pl.when(jnp.logical_not(stays(i, k)))
            def _():
                band_copy(i, k).wait_send()

        for step in range(1, N_TENSOR):
            y_copy(staged, from_y, step, i, send_y, recv_y).wait_send()
    own.wait()
    for i in range(3):
        for step in range(1, N_TENSOR):
            y_copy(to_y, land, step, i, send_z, recv_z).wait()

    to_row = one_hot(MATS * SUB, lambda o: (o % MATS) * SUB + o // MATS)
    by_row = permuted(to_row, land[...].reshape(MATS * SUB, WIDE))
    update_out[...] = jnp.concatenate([by_row[MATS * r:MATS * (r + 1), :HW] for r in range(SUB)], axis=1)
    tail = by_row[:MATS, WIDE - 128:].astype(f32)
    lane = lax.broadcasted_iota(jnp.int32, (MATS, 128), 1) - (HW - (WIDE - 128))
    matrix_rms = jnp.sum(jnp.where((lane == 0) | (lane == 1), tail, 0.0), axis=1, keepdims=True)
    slot = lax.broadcasted_iota(jnp.int32, (MATS, CAP), 1).astype(f32)
    rms_out[...] = jnp.sum(jnp.where(owned & (rank == slot), matrix_rms, 0.0), axis=0, keepdims=True)


def on_device(grad, momentum, owner):
    dma = pltpu.SemaphoreType.DMA
    band = (BAND, WIDE)
    by_y = (N_TENSOR, PER_Y * SUB, WIDE)
    vmem = pl.BlockSpec(memory_space=pltpu.VMEM)
    return pl.pallas_call(
        kernel,
        out_shape=(
            jax.ShapeDtypeStruct(momentum.shape, f32),
            jax.ShapeDtypeStruct(grad.shape, bf16),
            jax.ShapeDtypeStruct((1, CAP), f32),
        ),
        in_specs=[vmem] * 3,
        out_specs=[vmem] * 3,
        scratch_shapes=[
            pltpu.VMEM(by_y, bf16),
            pltpu.VMEM(by_y, bf16),
            pltpu.VMEM((PER_Y,) + band, bf16),
            pltpu.VMEM((PLANE,) + band, bf16),
            pltpu.VMEM((WIDE, ROWS), bf16),
            pltpu.VMEM((PLANE,) + band, bf16),
            pltpu.VMEM((PLANE,) + band, bf16),
            pltpu.VMEM((WIDE, WIDE), f32),
            pltpu.VMEM((2, WIDE // TILE, WIDE, TILE), bf16),
            pltpu.VMEM((2, WIDE // TILE, WIDE, TILE), bf16),
            pltpu.VMEM((WIDE, WIDE), bf16),
            pltpu.VMEM((WIDE, WIDE), bf16),
            pltpu.VMEM((PER_Y,) + band, bf16),
            pltpu.VMEM(by_y, bf16),
            pltpu.VMEM(by_y, bf16),
            dma((3, 3)), dma((3, 3)), dma((3, 4)), dma((4,)), dma((2, 3)), dma((2, 3)), dma, dma((3,)),
            dma((3, 3)), dma((3, 3)), dma, dma,
        ],
        compiler_params=pltpu.CompilerParams(
            collective_id=0, has_side_effects=True, vmem_limit_bytes=40 * 1024 * 1024
        ),
    )(grad, momentum, owner.reshape(1, MATS))


def solution(mesh):
    return jax.shard_map(
        on_device,
        mesh=mesh,
        in_specs=(P(None, ("dp", "tensor")), P(None, ("dp", "tensor")), P()),
        out_specs=(P(None, ("dp", "tensor")), P(None, ("dp", "tensor")), P("dp", None)),
        check_vma=False,
    )
```

time: 374 us -> 92.2 us (0.25)
  the two profiles are of different devices: /device:TPU:1 before, /device:TPU:52 now
where the time goes in v1:
time: 92.2 us; the launch traced here: 92 us
  Pallas kernels  86.7 us (94%)
  local copies, waits for them, and re-layouts  4.66 us (5%)
    pallas_call x1, Pallas kernels, on_device(): pl.pallas_call(kernel, out_shape=(jax.ShapeDtypeStruct(momentum.shape, f3...  86.7 us
    unnamed x9, local copies, waits for them, and re-layouts  4.66 us

profile of v1, /device:TPU:52, one launch (start us, length us, event | category | flops | bytes accessed | tf_op | source)
XLA Modules:
  0.0 92.0 jit_solution(419654225409564503)
XLA Ops:
  0.6 0.0 copy-start.2
  0.6 0.6 copy-done.2
  1.3 0.0 copy-start
  1.3 1.0 %copy-done = f32[48,2816]{1,0:T(8,128)S(1)} copy-done((f32[48,2816]{1,0:T(8,128)S(1)}, f32[48,2816]{1,0:T(8,128)}, u32[]{:S(2)}) %copy-start) | copy-done | bytes 540696
  2.3 0.0 copy-start.1
  2.3 1.0 %copy-done.1 = bf16[48,2816]{1,0:T(8,128)(2,1)S(1)} copy-done((bf16[48,2816]{1,0:T(8,128)(2,1)S(1)}, bf16[48,2816]{1,0:T(8,128)(2,1)}, u32[]{:S(2)}) %copy-start.1) | copy-done | bytes 270360
  3.3 86.7 %shard_map.58 = (f32[48,2816]{1,0:T(8,128)S(1)}, bf16[48,2816]{1,0:T(8,128)(2,1)S(1)}, f32[1,2]{1,0:T(1,128)S(1)}) custom-call(bf16[48,2816]{1,0:T(8,128)(2,1)S(1)} %copy-done.1, f32[48,2816]{1,0:T(8,128)S(1)} %copy-done, s32[1,48]{1,0:T(1,128)S(1)} %bitcast.1), custom_call_target="tpu_custom_call" | custom-call | tf_op jit(solution)/shard_map/pallas_call | solution.py:289
  90.0 0.8 copy.9
  90.8 0.7 copy.10
  91.5 0.5 copy.11
Async XLA Ops:
  0.6 0.7 copy-start.2
  1.3 1.0 %copy-start = (f32[48,2816]{1,0:T(8,128)S(1)}, f32[48,2816]{1,0:T(8,128)}, u32[]{:S(2)}) copy-start(f32[48,2816]{1,0:T(8,128)} %momentum_ref.1) | copy-start | bytes 1622020
  2.3 1.0 %copy-start.1 = (bf16[48,2816]{1,0:T(8,128)(2,1)S(1)}, bf16[48,2816]{1,0:T(8,128)(2,1)}, u32[]{:S(2)}) copy-start(bf16[48,2816]{1,0:T(8,128)(2,1)} %grad_ref.1) | copy-start | bytes 811012

commit v2 on v1

--- a/solution.py
+++ b/solution.py
@@ -31,8 +31,8 @@
 f32, bf16 = jnp.float32, jnp.bfloat16
 
 
-def home(j):
-    return (j % 4) * 16 + (j * 4) // 3
+def home(t, k):
+    return (k + 4 - t) % 4 * 16 + 4 * k + t
 
 
 def around(i):
@@ -52,14 +52,23 @@
 def kernel(
     grad_ref, momentum_ref, owner_ref, momentum_out, update_out, rms_out,
     staged, from_y, bands, rows, turned, mid, done, total, half, other, gram, poly, back, to_y, land,
-    send_y, recv_y, send_p, recv_p, send_g, recv_g, send_b, recv_b, send_z, recv_z, local_y, local_z,
+    grad_in, momentum_in, owner_in,
+    send_y, recv_y, send_p, recv_p, send_g, recv_g, send_b, recv_b, send_z, recv_z, local_y, local_z, loads,
 ):
     dp, y = lax.axis_index("dp"), lax.axis_index("tensor")
     core, place = dp % 2, dp // 2
     x, z = place // 16, place % 16
-    mine = (3 * z + 3) // 4
-    works = ((mine * 4) // 3 == z) & (mine % 4 == x) & (mine < PER_Y)
+    wave, spot = z % 4, z // 4
+    mine = 4 * wave + spot
+    works = (wave < 3) & ((spot + 4 - wave) % 4 == x)
     bands_per = TILE // BAND
+
+    fetches = [
+        pltpu.make_async_copy(src, dst, loads.at[n])
+        for n, (src, dst) in enumerate(((grad_ref, grad_in), (momentum_ref, momentum_in), (owner_ref, owner_in)))
+    ]
+    for fetch in fetches:
+        fetch.start()
 
     barrier = pltpu.get_barrier_semaphore()
     for step in range(1, N_TENSOR):
@@ -79,10 +88,13 @@
     @pl.when(jnp.logical_not(works))
     def _():
         for j in range(PER_Y):
-            pl.semaphore_signal(barrier, inc=1, device_id=(home(j) * 2 + core, y), device_id_type=MESH)
-
-    grad = grad_ref[...].astype(f32)
-    new_momentum = beta_decay * momentum_ref[...] + grad
+            pl.semaphore_signal(barrier, inc=1, device_id=(home(j // 4, j % 4) * 2 + core, y), device_id_type=MESH)
+
+    for fetch in fetches:
+        fetch.wait()
+
+    grad = grad_in[...].astype(f32)
+    new_momentum = beta_decay * momentum_in[...] + grad
     momentum_out[...] = new_momentum
     nesterov = (grad + beta_decay * new_momentum).astype(bf16)
     edge = jnp.zeros((MATS, WIDE - HW), bf16)
@@ -100,16 +112,14 @@
     def _():
         pl.semaphore_wait(barrier, N_TENSOR - 1 + PER_Y)
 
-    def tile_at(i):
-        t = (jnp.minimum(mine // 4, 2) + i) % 3
-        return t, pl.ds(pl.multiple_of(t * BAND, BAND), BAND)
-
-    def y_copy(src, dst, step, i, sends, recvs):
+    def wave_rows(t):
+        return pl.ds(t * BAND, BAND)
+
+    def y_copy(src, dst, step, t, sends, recvs):
         peer = (y + step) % N_TENSOR
-        at = tile_at(i)[1]
         return pltpu.make_async_remote_copy(
-            src_ref=src.at[peer, at], dst_ref=dst.at[y, at],
-            send_sem=sends.at[step - 1, i], recv_sem=recvs.at[step - 1, i],
+            src_ref=src.at[peer, wave_rows(t)], dst_ref=dst.at[y, wave_rows(t)],
+            send_sem=sends.at[step - 1, t], recv_sem=recvs.at[step - 1, t],
             device_id=(dp, peer), device_id_type=MESH,
         )
 
@@ -120,27 +130,30 @@
             y_copy(staged, from_y, step, i, send_y, recv_y).start()
     own.wait()
 
-    def band_copy(i, k):
-        j = tile_at(i)[0] * 4 + k
+    def band_copy(t, n):
+        k = (spot + (2, 1, 3, 0)[n]) % 4
         return pltpu.make_async_remote_copy(
-            src_ref=bands.at[j], dst_ref=rows.at[place], send_sem=send_p.at[i, k], recv_sem=recv_p.at[x],
-            device_id=(home(j) * 2 + core, y), device_id_type=MESH,
+            src_ref=bands.at[4 * t + k], dst_ref=rows.at[place], send_sem=send_p.at[t, n], recv_sem=recv_p.at[x],
+            device_id=(home(t, k) * 2 + core, y), device_id_type=MESH,
         )
 
-    def stays(i, k):
-        return works & (tile_at(i)[0] * 4 + k == mine)
+    def unless_mine(t, n, act):
+        if n < 3:
+            act()
+        else:
+            pl.when(jnp.logical_not(works & (wave == t)))(act)
 
     regroup = one_hot(4 * BAND, lambda o: (o // SUB % 4) * BAND + (o // BAND) * SUB + o % SUB)
-    for i in range(3):
-        for step in range(1, N_TENSOR):
-            y_copy(staged, from_y, step, i, send_y, recv_y).wait_recv()
-        t, at = tile_at(i)
-        tile = from_y[:, at, :].reshape(4 * BAND, WIDE)
+    for t in range(3):
+        for step in range(1, N_TENSOR):
+            y_copy(staged, from_y, step, t, send_y, recv_y).wait_recv()
+        tile = from_y[:, wave_rows(t), :].reshape(4 * BAND, WIDE)
         bands[pl.ds(4 * t, 4)] = permuted(regroup, tile).reshape(4, BAND, WIDE)
-        for k in range(4):
-            @pl.when(jnp.logical_not(stays(i, k)))
-            def _():
-                band_copy(i, k).start()
+        if t:
+            for n in range(4):
+                unless_mine(t - 1, n, lambda: band_copy(t - 1, n).wait_send())
+        for n in range(4):
+            unless_mine(t, n, lambda: band_copy(t, n).start())
 
     @pl.when(works)
     def _():
@@ -150,20 +163,35 @@
             at = pl.multiple_of(b * TILE, TILE)
             turned[:, pl.ds(at, TILE)] = ref[pl.ds(b * bands_per, bands_per)].reshape(TILE, WIDE).T
 
+        def upper(c):
+            return slice(0, (c + 1) * TILE), slice(c * TILE, (c + 1) * TILE)
+
         def swap(slot, c):
+            over = pl.ds(0, (c + 1) * TILE)
             return pltpu.make_async_remote_copy(
-                src_ref=half.at[slot, c], dst_ref=other.at[slot, c], send_sem=send_g.at[slot, c], recv_sem=recv_g.at[slot, c],
+                src_ref=half.at[slot, c, over], dst_ref=other.at[slot, c, over],
+                send_sem=send_g.at[slot, c], recv_sem=recv_g.at[slot, c],
                 device_id=(dp + 1 - 2 * core, y), device_id_type=MESH,
             )
 
         def gram_sum(ref, slot):
+            for c in (2, 1, 0):
+                over, across = upper(c)
+                right = ref[:, :, across].reshape(ROWS, TILE)
+                half[slot, c, over] = jnp.dot(turned[over], right, preferred_element_type=f32).astype(bf16)
+                swap(slot, c).start()
+            for c in (2, 1, 0):
+                swap(slot, c).wait()
+                over, across = upper(c)
+                total[over, across] = half[slot, c, over].astype(f32) + other[slot, c, over].astype(f32)
+
+        def set_gram(scale):
             for c in range(WIDE // TILE):
-                right = ref[:, :, c * TILE:(c + 1) * TILE].reshape(ROWS, TILE)
-                half[slot, c] = jnp.dot(turned[...], right, preferred_element_type=f32).astype(bf16)
-                swap(slot, c).start()
-            for c in range(WIDE // TILE):
-                swap(slot, c).wait()
-                total[:, c * TILE:(c + 1) * TILE] = half[slot, c].astype(f32) + other[slot, c].astype(f32)
+                over, across = upper(c)
+                block = (total[over, across] * scale * scale).astype(bf16)
+                gram[over, across] = block
+                for r in range(c):
+                    gram[across, r * TILE:(r + 1) * TILE] = block[r * TILE:(r + 1) * TILE].T
 
         def polynomial():
             current = gram[...]
@@ -185,21 +213,19 @@
         )
         squares = jnp.sum(jnp.sum(on_diagonal, axis=1, keepdims=True), axis=0, keepdims=True)
         inverse = 1.0 / (jnp.sqrt(squares) + epsilon)
-        gram[...] = (total[...] * inverse * inverse).astype(bf16)
+        set_gram(inverse)
         polynomial()
 
-        current = rows[...].reshape(ROWS, WIDE)
-        product = jnp.dot(current, poly[...], preferred_element_type=f32)
-        mixed = (coef_a * current.astype(f32) + product) * inverse
-        mid[...] = mixed.astype(bf16).reshape(PLANE, BAND, WIDE)
-
-        def turn_mid(b, carry):
-            turn(mid, b)
-            return carry
-
-        lax.fori_loop(0, ROWS // TILE, turn_mid, 0)
+        for b in range(ROWS // TILE):
+            at = slice(b * bands_per, (b + 1) * bands_per)
+            current = rows[at].reshape(TILE, WIDE)
+            product = jnp.dot(current, poly[...], preferred_element_type=f32)
+            mixed = ((coef_a * current.astype(f32) + product) * inverse).astype(bf16)
+            mid[at] = mixed.reshape(bands_per, BAND, WIDE)
+            turned[:, b * TILE:(b + 1) * TILE] = mixed.T
+
         gram_sum(mid, 1)
-        gram[...] = total[...].astype(bf16)
+        set_gram(1.0)
         polynomial()
 
         rms = jnp.sqrt(squares / (D * HW))
@@ -209,7 +235,7 @@
 
         def give(peer):
             return pltpu.make_async_remote_copy(
-                src_ref=done.at[peer], dst_ref=back.at[mine], send_sem=send_b, recv_sem=recv_b.at[mine // 4],
+                src_ref=done.at[peer], dst_ref=back.at[mine], send_sem=send_b, recv_sem=recv_b.at[wave],
                 device_id=(peer * 2 + core, y), device_id_type=MESH,
             )
 
@@ -233,23 +259,22 @@
             return carry
 
         lax.fori_loop(0, 2, finish, 0)
-        pltpu.make_async_copy(done.at[place], back.at[mine], recv_b.at[mine // 4]).start()
-
-    for i in range(3):
-        t, at = tile_at(i)
+        pltpu.make_async_copy(done.at[place], back.at[mine], recv_b.at[wave]).start()
+
+    for t in range(3):
         four = back.at[pl.ds(4 * t, 4)]
         pltpu.make_async_copy(four, four, recv_b.at[t]).wait()
         tile = back[pl.ds(4 * t, 4)].reshape(4 * BAND, WIDE)
-        to_y[:, at, :] = permuted(regroup, tile).reshape(4, BAND, WIDE)
-        for step in range(1, N_TENSOR):
-            y_copy(to_y, land, step, i, send_z, recv_z).start()
+        to_y[:, wave_rows(t), :] = permuted(regroup, tile).reshape(4, BAND, WIDE)
+        for step in range(1, N_TENSOR):
+            y_copy(to_y, land, step, t, send_z, recv_z).start()
 
     own = pltpu.make_async_copy(to_y.at[y], land.at[y], local_z)
     own.start()
 
     index_m = lax.broadcasted_iota(jnp.int32, (MATS, MATS), 0)
     index_n = lax.broadcasted_iota(jnp.int32, (MATS, MATS), 1)
-    owners = owner_ref[...].astype(f32)
+    owners = owner_in[...].astype(f32)
     owner = jnp.sum(jnp.where(index_m == index_n, owners, 0.0), axis=1, keepdims=True)
     rank = jnp.sum(jnp.where((owner == owners) & (index_n < index_m), 1.0, 0.0), axis=1, keepdims=True)
     owned = owner == dp.astype(f32)
@@ -259,10 +284,9 @@
         pltpu.make_async_copy(done.at[pl.ds(0, PLANE - 1)], done.at[pl.ds(0, PLANE - 1)], send_b).wait()
 
     for i in range(3):
-        for k in range(4):
-            @pl.when(jnp.logical_not(stays(i, k)))
-            def _():
-                band_copy(i, k).wait_send()
+        if i == 2:
+            for n in range(4):
+                unless_mine(i, n, lambda: band_copy(i, n).wait_send())
 
         for step in range(1, N_TENSOR):
             y_copy(staged, from_y, step, i, send_y, recv_y).wait_send()
@@ -293,7 +317,7 @@
             jax.ShapeDtypeStruct(grad.shape, bf16),
             jax.ShapeDtypeStruct((1, CAP), f32),
         ),
-        in_specs=[vmem] * 3,
+        in_specs=[pl.BlockSpec(memory_space=pltpu.HBM)] * 3,
         out_specs=[vmem] * 3,
         scratch_shapes=[
             pltpu.VMEM(by_y, bf16),
@@ -311,13 +335,16 @@
             pltpu.VMEM((PER_Y,) + band, bf16),
             pltpu.VMEM(by_y, bf16),
             pltpu.VMEM(by_y, bf16),
+            pltpu.VMEM(grad.shape, bf16),
+            pltpu.VMEM(momentum.shape, f32),
+            pltpu.VMEM((1, MATS), jnp.int32),
             dma((3, 3)), dma((3, 3)), dma((3, 4)), dma((4,)), dma((2, 3)), dma((2, 3)), dma, dma((3,)),
-            dma((3, 3)), dma((3, 3)), dma, dma,
+            dma((3, 3)), dma((3, 3)), dma, dma, dma((3,)),
         ],
         compiler_params=pltpu.CompilerParams(
             collective_id=0, has_side_effects=True, vmem_limit_bytes=40 * 1024 * 1024
         ),
-    )(grad, momentum, owner.reshape(1, MATS))
+    )(*(pltpu.with_memory_space_constraint(v, pltpu.HBM) for v in (grad, momentum, owner.reshape(1, MATS))))
 
 
 def solution(mesh):

time: 92.2 us -> 92 us (level)
  the two profiles are of different devices: /device:TPU:52 before, /device:TPU:1 now
where the time goes in v2:
time: 92 us; the launch traced here: 91.6 us
  Pallas kernels  88.9 us (97%)
  local copies, waits for them, and re-layouts  2.02 us (2%)
    pallas_call x1, Pallas kernels, on_device(): pl.pallas_call(kernel, out_shape=(jax.ShapeDtypeStruct(momentum.shape, f3...  88.9 us
    unnamed x3, local copies, waits for them, and re-layouts  2.02 us

profile of v2, /device:TPU:1, one launch (start us, length us, event | category | flops | bytes accessed | tf_op | source)
XLA Modules:
  0.0 91.6 jit_solution(3343884146993066866)
XLA Ops:
  0.6 88.9 %shard_map.58 = (f32[48,2816]{1,0:T(8,128)S(1)}, bf16[48,2816]{1,0:T(8,128)(2,1)S(1)}, f32[1,2]{1,0:T(1,128)S(1)}) custom-call(bf16[48,2816]{1,0:T(8,128)(2,1)} %grad_ref.1, f32[48,2816]{1,0:T(8,128)} %momentum_ref.1, s32[1,48]{1,0:T(1,128)} %bitcast.1), custom_call_target="tpu_custom_call" | custom-call | tf_op jit(solution)/shard_map/pallas_call | solution.py:313
  89.5 0.8 copy.9
  90.3 0.7 copy.10
  91.1 0.5 copy.11

commit v3 on v2

--- a/solution.py
+++ b/solution.py
@@ -31,8 +31,8 @@
 f32, bf16 = jnp.float32, jnp.bfloat16
 
 
-def home(t, k):
-    return (k + 4 - t) % 4 * 16 + 4 * k + t
+def home(j):
+    return (j % 4) * 16 + (j * 4) // 3
 
 
 def around(i):
@@ -58,9 +58,8 @@
     dp, y = lax.axis_index("dp"), lax.axis_index("tensor")
     core, place = dp % 2, dp // 2
     x, z = place // 16, place % 16
-    wave, spot = z % 4, z // 4
-    mine = 4 * wave + spot
-    works = (wave < 3) & ((spot + 4 - wave) % 4 == x)
+    mine = (3 * z + 3) // 4
+    works = ((mine * 4) // 3 == z) & (mine % 4 == x) & (mine < PER_Y)
     bands_per = TILE // BAND
 
     fetches = [
@@ -79,16 +78,23 @@
         pl.semaphore_signal(barrier, inc=1, device_id=(dp + 1 - 2 * core, y), device_id_type=MESH)
 
         def greet(step, carry):
-            peer = (place + step) % PLANE
-            pl.semaphore_signal(barrier, inc=1, device_id=(peer * 2 + core, y), device_id_type=MESH)
+            column = (x + step) % 4
+            for n in range(15):
+                peer = column * 16 + (z + 8 + around(n)) % 16
+                pl.semaphore_signal(barrier, inc=1, device_id=(peer * 2 + core, y), device_id_type=MESH)
+
+            @pl.when(column != x)
+            def _():
+                pl.semaphore_signal(barrier, inc=1, device_id=((column * 16 + z) * 2 + core, y), device_id_type=MESH)
+
             return carry
 
-        lax.fori_loop(1, PLANE, greet, 0)
+        lax.fori_loop(1, 5, greet, 0)
 
     @pl.when(jnp.logical_not(works))
     def _():
         for j in range(PER_Y):
-            pl.semaphore_signal(barrier, inc=1, device_id=(home(j // 4, j % 4) * 2 + core, y), device_id_type=MESH)
+            pl.semaphore_signal(barrier, inc=1, device_id=(home(j) * 2 + core, y), device_id_type=MESH)
 
     for fetch in fetches:
         fetch.wait()
@@ -112,14 +118,16 @@
     def _():
         pl.semaphore_wait(barrier, N_TENSOR - 1 + PER_Y)
 
-    def wave_rows(t):
-        return pl.ds(t * BAND, BAND)
-
-    def y_copy(src, dst, step, t, sends, recvs):
+    def tile_at(i):
+        t = (jnp.minimum(mine // 4, 2) + i) % 3
+        return t, pl.ds(pl.multiple_of(t * BAND, BAND), BAND)
+
+    def y_copy(src, dst, step, i, sends, recvs):
         peer = (y + step) % N_TENSOR
+        at = tile_at(i)[1]
         return pltpu.make_async_remote_copy(
-            src_ref=src.at[peer, wave_rows(t)], dst_ref=dst.at[y, wave_rows(t)],
-            send_sem=sends.at[step - 1, t], recv_sem=recvs.at[step - 1, t],
+            src_ref=src.at[peer, at], dst_ref=dst.at[y, at],
+            send_sem=sends.at[step - 1, i], recv_sem=recvs.at[step - 1, i],
             device_id=(dp, peer), device_id_type=MESH,
         )
 
@@ -130,30 +138,27 @@
             y_copy(staged, from_y, step, i, send_y, recv_y).start()
     own.wait()
 
-    def band_copy(t, n):
-        k = (spot + (2, 1, 3, 0)[n]) % 4
+    def band_copy(i, k):
+        j = tile_at(i)[0] * 4 + k
         return pltpu.make_async_remote_copy(
-            src_ref=bands.at[4 * t + k], dst_ref=rows.at[place], send_sem=send_p.at[t, n], recv_sem=recv_p.at[x],
-            device_id=(home(t, k) * 2 + core, y), device_id_type=MESH,
+            src_ref=bands.at[j], dst_ref=rows.at[place], send_sem=send_p.at[i, k], recv_sem=recv_p.at[x],
+            device_id=(home(j) * 2 + core, y), device_id_type=MESH,
         )
 
-    def unless_mine(t, n, act):
-        if n < 3:
-            act()
-        else:
-            pl.when(jnp.logical_not(works & (wave == t)))(act)
+    def stays(i, k):
+        return works & (tile_at(i)[0] * 4 + k == mine)
 
     regroup = one_hot(4 * BAND, lambda o: (o // SUB % 4) * BAND + (o // BAND) * SUB + o % SUB)
-    for t in range(3):
-        for step in range(1, N_TENSOR):
-            y_copy(staged, from_y, step, t, send_y, recv_y).wait_recv()
-        tile = from_y[:, wave_rows(t), :].reshape(4 * BAND, WIDE)
+    for i in range(3):
+        for step in range(1, N_TENSOR):
+            y_copy(staged, from_y, step, i, send_y, recv_y).wait_recv()
+        t, at = tile_at(i)
+        tile = from_y[:, at, :].reshape(4 * BAND, WIDE)
         bands[pl.ds(4 * t, 4)] = permuted(regroup, tile).reshape(4, BAND, WIDE)
-        if t:
-            for n in range(4):
-                unless_mine(t - 1, n, lambda: band_copy(t - 1, n).wait_send())
-        for n in range(4):
-            unless_mine(t, n, lambda: band_copy(t, n).start())
+        for k in range(4):
+            @pl.when(jnp.logical_not(stays(i, k)))
+            def _():
+                band_copy(i, k).start()
 
     @pl.when(works)
     def _():
@@ -235,7 +240,7 @@
 
         def give(peer):
             return pltpu.make_async_remote_copy(
-                src_ref=done.at[peer], dst_ref=back.at[mine], send_sem=send_b, recv_sem=recv_b.at[wave],
+                src_ref=done.at[peer], dst_ref=back.at[mine], send_sem=send_b, recv_sem=recv_b.at[mine // 4],
                 device_id=(peer * 2 + core, y), device_id_type=MESH,
             )
 
@@ -259,15 +264,16 @@
             return carry
 
         lax.fori_loop(0, 2, finish, 0)
-        pltpu.make_async_copy(done.at[place], back.at[mine], recv_b.at[wave]).start()
-
-    for t in range(3):
+        pltpu.make_async_copy(done.at[place], back.at[mine], recv_b.at[mine // 4]).start()
+
+    for i in range(3):
+        t, at = tile_at(i)
         four = back.at[pl.ds(4 * t, 4)]
         pltpu.make_async_copy(four, four, recv_b.at[t]).wait()
         tile = back[pl.ds(4 * t, 4)].reshape(4 * BAND, WIDE)
-        to_y[:, wave_rows(t), :] = permuted(regroup, tile).reshape(4, BAND, WIDE)
-        for step in range(1, N_TENSOR):
-            y_copy(to_y, land, step, t, send_z, recv_z).start()
+        to_y[:, at, :] = permuted(regroup, tile).reshape(4, BAND, WIDE)
+        for step in range(1, N_TENSOR):
+            y_copy(to_y, land, step, i, send_z, recv_z).start()
 
     own = pltpu.make_async_copy(to_y.at[y], land.at[y], local_z)
     own.start()
@@ -284,9 +290,10 @@
         pltpu.make_async_copy(done.at[pl.ds(0, PLANE - 1)], done.at[pl.ds(0, PLANE - 1)], send_b).wait()
 
     for i in range(3):
-        if i == 2:
-            for n in range(4):
-                unless_mine(i, n, lambda: band_copy(i, n).wait_send())
+        for k in range(4):
+            @pl.when(jnp.logical_not(stays(i, k)))
+            def _():
+                band_copy(i, k).wait_send()
 
         for step in range(1, N_TENSOR):
             y_copy(staged, from_y, step, i, send_y, recv_y).wait_send()

time: 92 us -> 86.2 us (0.937)
  the two profiles are of different devices: /device:TPU:1 before, /device:TPU:66 now
where the time goes in v3:
time: 86.2 us; the launch traced here: 86.1 us
  Pallas kernels  83.4 us (97%)
  local copies, waits for them, and re-layouts  2.02 us (2%)
    pallas_call x1, Pallas kernels, on_device(): pl.pallas_call(kernel, out_shape=(jax.ShapeDtypeStruct(momentum.shape, f3...  83.4 us
    unnamed x3, local copies, waits for them, and re-layouts  2.02 us

profile of v3, /device:TPU:66, one launch (start us, length us, event | category | flops | bytes accessed | tf_op | source)
XLA Modules:
  0.0 86.1 jit_solution(14302604869877559680)
XLA Ops:
  0.6 83.4 %shard_map.58 = (f32[48,2816]{1,0:T(8,128)S(1)}, bf16[48,2816]{1,0:T(8,128)(2,1)S(1)}, f32[1,2]{1,0:T(1,128)S(1)}) custom-call(bf16[48,2816]{1,0:T(8,128)(2,1)} %grad_ref.1, f32[48,2816]{1,0:T(8,128)} %momentum_ref.1, s32[1,48]{1,0:T(1,128)} %bitcast.1), custom_call_target="tpu_custom_call" | custom-call | tf_op jit(solution)/shard_map/pallas_call | solution.py:320
  84.0 0.8 copy.9
  84.9 0.7 copy.10
  85.6 0.5 copy.11

commit v4 on v3

--- a/solution.py
+++ b/solution.py
@@ -119,7 +119,8 @@
         pl.semaphore_wait(barrier, N_TENSOR - 1 + PER_Y)
 
     def tile_at(i):
-        t = (jnp.minimum(mine // 4, 2) + i) % 3
+        near = jnp.minimum(mine, PER_Y - 1)
+        t = (near // 4 + 3 + i * jnp.where(near % 4 >= 2, 1, -1)) % 3
         return t, pl.ds(pl.multiple_of(t * BAND, BAND), BAND)
 
     def y_copy(src, dst, step, i, sends, recvs):
@@ -252,7 +253,7 @@
             mixed = (coef_a * current.astype(f32) + product) * math.sqrt(max(D, HW))
             mixed = jnp.where(lane == HW, high, jnp.where(lane == HW + 1, low, mixed))
             done[at] = mixed.astype(bf16).reshape(2 * bands_per, BAND, WIDE)
-            for k in range(16):
+            for k in reversed(range(16)):
                 for h in range(2):
                     peer = (pair * 2 + h) * 16 + (z + 16 + around(k)) % 16
                     if k:
@@ -266,7 +267,7 @@
         lax.fori_loop(0, 2, finish, 0)
         pltpu.make_async_copy(done.at[place], back.at[mine], recv_b.at[mine // 4]).start()
 
-    for i in range(3):
+    for i in (2, 1, 0):
         t, at = tile_at(i)
         four = back.at[pl.ds(4 * t, 4)]
         pltpu.make_async_copy(four, four, recv_b.at[t]).wait()

time: 86.2 us -> 83.3 us (0.966)
  the two profiles are of different devices: /device:TPU:66 before, /device:TPU:1 now
where the time goes in v4:
time: 83.3 us; the launch traced here: 81.7 us
  Pallas kernels  79.1 us (95%)
  local copies, waits for them, and re-layouts  2.02 us (2%)
    pallas_call x1, Pallas kernels, on_device(): pl.pallas_call(kernel, out_shape=(jax.ShapeDtypeStruct(momentum.shape, f3...  79.1 us
    unnamed x3, local copies, waits for them, and re-layouts  2.02 us

profile of v4, /device:TPU:1, one launch (start us, length us, event | category | flops | bytes accessed | tf_op | source)
XLA Modules:
  0.0 81.7 jit_solution(5694484440134184767)
XLA Ops:
  0.6 79.1 %shard_map.58 = (f32[48,2816]{1,0:T(8,128)S(1)}, bf16[48,2816]{1,0:T(8,128)(2,1)S(1)}, f32[1,2]{1,0:T(1,128)S(1)}) custom-call(bf16[48,2816]{1,0:T(8,128)(2,1)} %grad_ref.1, f32[48,2816]{1,0:T(8,128)} %momentum_ref.1, s32[1,48]{1,0:T(1,128)} %bitcast.1), custom_call_target="tpu_custom_call" | custom-call | tf_op jit(solution)/shard_map/pallas_call | solution.py:321
  79.7 0.8 copy.9
  80.5 0.7 copy.10
  81.2 0.5 copy.11

commit v5 on v4

--- a/solution.py
+++ b/solution.py
@@ -58,6 +58,7 @@
     dp, y = lax.axis_index("dp"), lax.axis_index("tensor")
     core, place = dp % 2, dp // 2
     x, z = place // 16, place % 16
+    slot = z * 4 + x
     mine = (3 * z + 3) // 4
     works = ((mine * 4) // 3 == z) & (mine % 4 == x) & (mine < PER_Y)
     bands_per = TILE // BAND
@@ -142,7 +143,7 @@
     def band_copy(i, k):
         j = tile_at(i)[0] * 4 + k
         return pltpu.make_async_remote_copy(
-            src_ref=bands.at[j], dst_ref=rows.at[place], send_sem=send_p.at[i, k], recv_sem=recv_p.at[x],
+            src_ref=bands.at[j], dst_ref=rows.at[slot], send_sem=send_p.at[i, k], recv_sem=recv_p.at[z // 4],
             device_id=(home(j) * 2 + core, y), device_id_type=MESH,
         )
 
@@ -163,33 +164,34 @@
 
     @pl.when(works)
     def _():
-        pltpu.make_async_copy(bands.at[mine], rows.at[place], recv_p.at[x]).start()
-
-        def turn(ref, b):
-            at = pl.multiple_of(b * TILE, TILE)
-            turned[:, pl.ds(at, TILE)] = ref[pl.ds(b * bands_per, bands_per)].reshape(TILE, WIDE).T
+        pltpu.make_async_copy(bands.at[mine], rows.at[slot], recv_p.at[z // 4]).start()
+
+        def quarter(d):
+            return (z // 4 + d) % 4
+
+        def bands_of(d):
+            return pl.ds(quarter(d) * bands_per, bands_per)
 
         def upper(c):
             return slice(0, (c + 1) * TILE), slice(c * TILE, (c + 1) * TILE)
 
-        def swap(slot, c):
+        def swap(turn, c):
             over = pl.ds(0, (c + 1) * TILE)
             return pltpu.make_async_remote_copy(
-                src_ref=half.at[slot, c, over], dst_ref=other.at[slot, c, over],
-                send_sem=send_g.at[slot, c], recv_sem=recv_g.at[slot, c],
+                src_ref=half.at[turn, c, over], dst_ref=other.at[turn, c, over],
+                send_sem=send_g.at[turn, c], recv_sem=recv_g.at[turn, c],
                 device_id=(dp + 1 - 2 * core, y), device_id_type=MESH,
             )
 
-        def gram_sum(ref, slot):
+        def give_half(turn, c, value):
+            half[turn, c, upper(c)[0]] = value.astype(bf16)
+            swap(turn, c).start()
+
+        def gram_sum(turn):
             for c in (2, 1, 0):
+                swap(turn, c).wait()
                 over, across = upper(c)
-                right = ref[:, :, across].reshape(ROWS, TILE)
-                half[slot, c, over] = jnp.dot(turned[over], right, preferred_element_type=f32).astype(bf16)
-                swap(slot, c).start()
-            for c in (2, 1, 0):
-                swap(slot, c).wait()
-                over, across = upper(c)
-                total[over, across] = half[slot, c, over].astype(f32) + other[slot, c, over].astype(f32)
+                total[over, across] = half[turn, c, over].astype(f32) + other[turn, c, over].astype(f32)
 
         def set_gram(scale):
             for c in range(WIDE // TILE):
@@ -204,15 +206,25 @@
             square = jnp.dot(current, current, preferred_element_type=f32)
             poly[...] = (coef_b * current.astype(f32) + coef_c * square).astype(bf16)
 
-        def arrive(i, carry):
-            b = (x + i) % 4
-            column = rows.at[pl.ds(b * bands_per, bands_per)]
-            pltpu.make_async_copy(column, column, recv_p.at[b]).wait()
-            turn(rows, b)
-            return carry
-
-        lax.fori_loop(0, ROWS // TILE, arrive, 0)
-        gram_sum(rows, 0)
+        for ds in ((0,), (1, 3), (2,)):
+            for d in ds:
+                part = rows.at[bands_of(d)]
+                pltpu.make_async_copy(part, part, recv_p.at[quarter(d)]).wait()
+                at = pl.multiple_of(quarter(d) * TILE, TILE)
+                turned[:, pl.ds(at, TILE)] = rows[bands_of(d)].reshape(TILE, WIDE).T
+            for c in (2, 1, 0):
+                over, across = upper(c)
+                value = total[over, across] if ds[0] else 0.0
+                for d in ds:
+                    at = pl.multiple_of(quarter(d) * TILE, TILE)
+                    right = rows[bands_of(d), :, across].reshape(TILE, TILE)
+                    value += jnp.dot(turned[over, pl.ds(at, TILE)], right, preferred_element_type=f32)
+                if ds[0] == 2:
+                    give_half(0, c, value)
+                else:
+                    total[over, across] = value
+
+        gram_sum(0)
         diagonal = lax.broadcasted_iota(jnp.int32, (TILE, TILE), 0) == lax.broadcasted_iota(jnp.int32, (TILE, TILE), 1)
         on_diagonal = sum(
             jnp.where(diagonal, total[c * TILE:(c + 1) * TILE, c * TILE:(c + 1) * TILE], 0.0) for c in range(WIDE // TILE)
@@ -230,42 +242,40 @@
             mid[at] = mixed.reshape(bands_per, BAND, WIDE)
             turned[:, b * TILE:(b + 1) * TILE] = mixed.T
 
-        gram_sum(mid, 1)
+        for c in (2, 1, 0):
+            over, across = upper(c)
+            right = mid[:, :, across].reshape(ROWS, TILE)
+            give_half(1, c, jnp.dot(turned[over], right, preferred_element_type=f32))
+        gram_sum(1)
         set_gram(1.0)
         polynomial()
 
         rms = jnp.sqrt(squares / (D * HW))
         high = rms.astype(bf16).astype(f32)
         low = rms - high
-        lane = lax.broadcasted_iota(jnp.int32, (2 * TILE, WIDE), 1)
-
-        def give(peer):
+        def give(peer_x, peer_z):
             return pltpu.make_async_remote_copy(
-                src_ref=done.at[peer], dst_ref=back.at[mine], send_sem=send_b, recv_sem=recv_b.at[mine // 4],
-                device_id=(peer * 2 + core, y), device_id_type=MESH,
+                src_ref=done.at[peer_z * 4 + peer_x], dst_ref=back.at[mine], send_sem=send_b, recv_sem=recv_b.at[mine // 4],
+                device_id=((peer_x * 16 + peer_z) * 2 + core, y), device_id_type=MESH,
             )
 
-        def finish(i, carry):
-            pair = (x // 2 + 1 + i) % 2
-            at = pl.ds(pair * 2 * bands_per, 2 * bands_per)
-            current = mid[at].reshape(2 * TILE, WIDE)
+        far = [(2, r) for r in (1, 2, 0, 3)]
+        sides = [pair for n in range(4) for pair in ((1, 3 - n), (3, n))]
+        own = [(0, (z + n) % 4) for n in (2, 3, 1, 0)]
+        for ds, peers in (((2,), far), ((1, 3), sides), ((0,), own)):
+            current = jnp.concatenate([mid[bands_of(d)].reshape(TILE, WIDE) for d in ds], axis=0)
+            lane = lax.broadcasted_iota(jnp.int32, current.shape, 1)
             product = jnp.dot(current, poly[...], preferred_element_type=f32)
             mixed = (coef_a * current.astype(f32) + product) * math.sqrt(max(D, HW))
-            mixed = jnp.where(lane == HW, high, jnp.where(lane == HW + 1, low, mixed))
-            done[at] = mixed.astype(bf16).reshape(2 * bands_per, BAND, WIDE)
-            for k in reversed(range(16)):
-                for h in range(2):
-                    peer = (pair * 2 + h) * 16 + (z + 16 + around(k)) % 16
-                    if k:
-                        give(peer).start()
-                    else:
-                        @pl.when(peer != place)
-                        def _():
-                            give(peer).start()
-            return carry
-
-        lax.fori_loop(0, 2, finish, 0)
-        pltpu.make_async_copy(done.at[place], back.at[mine], recv_b.at[mine // 4]).start()
+            mixed = jnp.where(lane == HW, high, jnp.where(lane == HW + 1, low, mixed)).astype(bf16)
+            for n, d in enumerate(ds):
+                done[bands_of(d)] = mixed[n * TILE:(n + 1) * TILE].reshape(bands_per, BAND, WIDE)
+            for n, (d, r) in enumerate(peers):
+                for h in (2, 1, 3, 0):
+                    if d or n < 3 or h:
+                        give((x + h) % 4, quarter(d) * 4 + r).start()
+
+        pltpu.make_async_copy(done.at[slot], back.at[mine], recv_b.at[mine // 4]).start()
 
     for i in (2, 1, 0):
         t, at = tile_at(i)
@@ -309,8 +319,8 @@
     tail = by_row[:MATS, WIDE - 128:].astype(f32)
     lane = lax.broadcasted_iota(jnp.int32, (MATS, 128), 1) - (HW - (WIDE - 128))
     matrix_rms = jnp.sum(jnp.where((lane == 0) | (lane == 1), tail, 0.0), axis=1, keepdims=True)
-    slot = lax.broadcasted_iota(jnp.int32, (MATS, CAP), 1).astype(f32)
-    rms_out[...] = jnp.sum(jnp.where(owned & (rank == slot), matrix_rms, 0.0), axis=0, keepdims=True)
+    ranks = lax.broadcasted_iota(jnp.int32, (MATS, CAP), 1).astype(f32)
+    rms_out[...] = jnp.sum(jnp.where(owned & (rank == ranks), matrix_rms, 0.0), axis=0, keepdims=True)
 
 
 def on_device(grad, momentum, owner):

time: 83.3 us -> 80.7 us (0.969); the launches traced: 81.7 us -> 80.5 us
  Pallas kernels: 79.1 us -> 77.9 us
    pallas_call x1, Pallas kernels: 79.1 us -> 77.9 us  [on_device(): pl.pallas_call(kernel, out_shape=(jax.ShapeDtypeStruct(momentum.shape, f3...]
where the time goes in v5:
time: 80.7 us; the launch traced here: 80.5 us
  Pallas kernels  77.9 us (97%)
  local copies, waits for them, and re-layouts  2.02 us (3%)
    pallas_call x1, Pallas kernels, on_device(): pl.pallas_call(kernel, out_shape=(jax.ShapeDtypeStruct(momentum.shape, f3...  77.9 us
    unnamed x3, local copies, waits for them, and re-layouts  2.02 us

profile of v5, /device:TPU:1, one launch (start us, length us, event | category | flops | bytes accessed | tf_op | source)
XLA Modules:
  0.0 80.5 jit_solution(14320992083796834103)
XLA Ops:
  0.6 77.9 %shard_map.58 = (f32[48,2816]{1,0:T(8,128)S(1)}, bf16[48,2816]{1,0:T(8,128)(2,1)S(1)}, f32[1,2]{1,0:T(1,128)S(1)}) custom-call(bf16[48,2816]{1,0:T(8,128)(2,1)} %grad_ref.1, f32[48,2816]{1,0:T(8,128)} %momentum_ref.1, s32[1,48]{1,0:T(1,128)} %bitcast.1), custom_call_target="tpu_custom_call" | custom-call | tf_op jit(solution)/shard_map/pallas_call | solution.py:331
  78.5 0.8 copy.9
  79.3 0.7 copy.10
  80.0 0.5 copy.11

commit v6 on v5

--- a/solution.py
+++ b/solution.py
@@ -119,9 +119,11 @@
     def _():
         pl.semaphore_wait(barrier, N_TENSOR - 1 + PER_Y)
 
+    near = jnp.minimum(mine, PER_Y - 1)
+    upward = near % 4 >= 2
+
     def tile_at(i):
-        near = jnp.minimum(mine, PER_Y - 1)
-        t = (near // 4 + 3 + i * jnp.where(near % 4 >= 2, 1, -1)) % 3
+        t = (near // 4 + 3 + i * jnp.where(upward, 1, -1)) % 3
         return t, pl.ds(pl.multiple_of(t * BAND, BAND), BAND)
 
     def y_copy(src, dst, step, i, sends, recvs):
@@ -140,15 +142,22 @@
             y_copy(staged, from_y, step, i, send_y, recv_y).start()
     own.wait()
 
-    def band_copy(i, k):
-        j = tile_at(i)[0] * 4 + k
+    def matrix_at(i, n):
+        k = n if i == 0 else jnp.where(upward == (i == 1), n, 3 - n)
+        return tile_at(i)[0] * 4 + k
+
+    def band_copy(i, n):
+        j = matrix_at(i, n)
         return pltpu.make_async_remote_copy(
-            src_ref=bands.at[j], dst_ref=rows.at[slot], send_sem=send_p.at[i, k], recv_sem=recv_p.at[z // 4],
+            src_ref=bands.at[j], dst_ref=rows.at[slot], send_sem=send_p.at[i, n], recv_sem=recv_p.at[z // 4],
             device_id=(home(j) * 2 + core, y), device_id_type=MESH,
         )
 
-    def stays(i, k):
-        return works & (tile_at(i)[0] * 4 + k == mine)
+    def unless_mine(i, n, act):
+        if i:
+            act()
+        else:
+            pl.when(jnp.logical_not(works & (matrix_at(0, n) == mine)))(act)
 
     regroup = one_hot(4 * BAND, lambda o: (o // SUB % 4) * BAND + (o // BAND) * SUB + o % SUB)
     for i in range(3):
@@ -157,10 +166,12 @@
         t, at = tile_at(i)
         tile = from_y[:, at, :].reshape(4 * BAND, WIDE)
         bands[pl.ds(4 * t, 4)] = permuted(regroup, tile).reshape(4, BAND, WIDE)
-        for k in range(4):
-            @pl.when(jnp.logical_not(stays(i, k)))
-            def _():
-                band_copy(i, k).start()
+        if i == 0:
+            for n in range(4):
+                unless_mine(0, n, lambda: band_copy(0, n).start())
+    for n in range(4):
+        for i in (1, 2):
+            band_copy(i, n).start()
 
     @pl.when(works)
     def _():
@@ -301,10 +312,8 @@
         pltpu.make_async_copy(done.at[pl.ds(0, PLANE - 1)], done.at[pl.ds(0, PLANE - 1)], send_b).wait()
 
     for i in range(3):
-        for k in range(4):
-            @pl.when(jnp.logical_not(stays(i, k)))
-            def _():
-                band_copy(i, k).wait_send()
+        for n in range(4):
+            unless_mine(i, n, lambda: band_copy(i, n).wait_send())
 
         for step in range(1, N_TENSOR):
             y_copy(staged, from_y, step, i, send_y, recv_y).wait_send()

time: 80.7 us -> 81.7 us (1.012)
  Pallas kernels: 77.9 us -> 78.9 us
    pallas_call x1, Pallas kernels: 77.9 us -> 78.9 us  [on_device(): pl.pallas_call(kernel, out_shape=(jax.ShapeDtypeStruct(momentum.shape, f3...]
where the time goes in v6:
time: 81.7 us; the launch traced here: 81.5 us
  Pallas kernels  78.9 us (97%)
  local copies, waits for them, and re-layouts  2.02 us (2%)
    pallas_call x1, Pallas kernels, on_device(): pl.pallas_call(kernel, out_shape=(jax.ShapeDtypeStruct(momentum.shape, f3...  78.9 us
    unnamed x3, local copies, waits for them, and re-layouts  2.02 us

profile of v6, /device:TPU:1, one launch (start us, length us, event | category | flops | bytes accessed | tf_op | source)
XLA Modules:
  0.0 81.5 jit_solution(6527044157318274595)
XLA Ops:
  0.6 78.9 %shard_map.58 = (f32[48,2816]{1,0:T(8,128)S(1)}, bf16[48,2816]{1,0:T(8,128)(2,1)S(1)}, f32[1,2]{1,0:T(1,128)S(1)}) custom-call(bf16[48,2816]{1,0:T(8,128)(2,1)} %grad_ref.1, f32[48,2816]{1,0:T(8,128)} %momentum_ref.1, s32[1,48]{1,0:T(1,128)} %bitcast.1), custom_call_target="tpu_custom_call" | custom-call | tf_op jit(solution)/shard_map/pallas_call | solution.py:340
  79.5 0.8 copy.9
  80.3 0.7 copy.10
  81.0 0.5 copy.11

commit v7 on v5

--- a/solution.py
+++ b/solution.py
@@ -323,18 +323,27 @@
     rms_out[...] = jnp.sum(jnp.where(owned & (rank == ranks), matrix_rms, 0.0), axis=0, keepdims=True)
 
 
+def write_out(*refs):
+    copies = [pltpu.make_async_copy(refs[n], refs[n + 3], refs[6].at[n]) for n in range(3)]
+    for copy in copies:
+        copy.start()
+    for copy in copies:
+        copy.wait()
+
+
 def on_device(grad, momentum, owner):
     dma = pltpu.SemaphoreType.DMA
     band = (BAND, WIDE)
     by_y = (N_TENSOR, PER_Y * SUB, WIDE)
     vmem = pl.BlockSpec(memory_space=pltpu.VMEM)
-    return pl.pallas_call(
+    shapes = (
+        jax.ShapeDtypeStruct(momentum.shape, f32),
+        jax.ShapeDtypeStruct(grad.shape, bf16),
+        jax.ShapeDtypeStruct((1, CAP), f32),
+    )
+    results = pl.pallas_call(
         kernel,
-        out_shape=(
-            jax.ShapeDtypeStruct(momentum.shape, f32),
-            jax.ShapeDtypeStruct(grad.shape, bf16),
-            jax.ShapeDtypeStruct((1, CAP), f32),
-        ),
+        out_shape=shapes,
         in_specs=[pl.BlockSpec(memory_space=pltpu.HBM)] * 3,
         out_specs=[vmem] * 3,
         scratch_shapes=[
@@ -363,6 +372,13 @@
             collective_id=0, has_side_effects=True, vmem_limit_bytes=40 * 1024 * 1024
         ),
     )(*(pltpu.with_memory_space_constraint(v, pltpu.HBM) for v in (grad, momentum, owner.reshape(1, MATS))))
+    return pl.pallas_call(
+        write_out,
+        out_shape=shapes,
+        in_specs=[vmem] * 3,
+        out_specs=[pl.BlockSpec(memory_space=pl.ANY)] * 3,
+        scratch_shapes=[dma((3,))],
+    )(*results)
 
 
 def solution(mesh):

time: 80.7 us -> 82.7 us (1.025)
  Pallas kernels: 77.9 us -> 79.9 us
    pallas_call x1 -> x2, Pallas kernels: 77.9 us -> 79.9 us  [the longest x1 77.9 us: on_device(): pl.pallas_call(kernel, out_shape=shapes, in_specs=[pl.BlockSpec(memory_sp...]
    unnamed x3 -> x6, local copies, waits for them, and re-layouts: 2.02 us -> 2 us
where the time goes in v7:
time: 82.7 us; the launch traced here: 82.6 us
  Pallas kernels  79.9 us (97%)
  local copies, waits for them, and re-layouts  2 us (2%)
    pallas_call x1, Pallas kernels, on_device(): pl.pallas_call(kernel, out_shape=shapes, in_specs=[pl.BlockSpec(memory_sp...  77.9 us
    pallas_call x1, Pallas kernels, on_device(): pl.pallas_call(write_out, out_shape=shapes, in_specs=[vmem] * 3, out_spec...  2.04 us
    unnamed x6, local copies, waits for them, and re-layouts  2 us

profile of v7, /device:TPU:1, one launch (start us, length us, event | category | flops | bytes accessed | tf_op | source)
XLA Modules:
  0.0 82.6 jit_solution(14697228353990936928)
XLA Ops:
  0.6 77.9 %shard_map.58 = (f32[48,2816]{1,0:T(8,128)S(1)}, bf16[48,2816]{1,0:T(8,128)(2,1)S(1)}, f32[1,2]{1,0:T(1,128)S(1)}) custom-call(bf16[48,2816]{1,0:T(8,128)(2,1)} %grad_ref.1, f32[48,2816]{1,0:T(8,128)} %momentum_ref.1, s32[1,48]{1,0:T(1,128)} %bitcast.1), custom_call_target="tpu_custom_call" | custom-call | tf_op jit(solution)/shard_map/pallas_call | solution.py:344
  78.5 0.0 copy-start
  78.5 0.8 copy-done
  79.3 0.0 copy-start.1
  79.3 0.7 copy-done.1
  80.0 0.0 copy-start.2
  80.0 0.5 copy-done.2
  80.5 2.0 %shard_map.59 = (f32[48,2816]{1,0:T(8,128)}, bf16[48,2816]{1,0:T(8,128)(2,1)}, f32[1,2]{1,0:T(1,128)}) custom-call(f32[48,2816]{1,0:T(8,128)} %copy-done, bf16[48,2816]{1,0:T(8,128)(2,1)} %copy-done.1, f32[1,2]{1,0:T(1,128)} %copy-done.2), custom_call_target="tpu_custom_call" | custom-call | tf_op jit(solution)/shard_map/pallas_call | solution.py:375
Async XLA Ops:
  78.5 0.8 copy-start
  79.3 0.7 copy-start.1
  80.0 0.5 copy-start.2

commit v8 on v5

--- a/solution.py
+++ b/solution.py
@@ -78,19 +78,11 @@
     def _():
         pl.semaphore_signal(barrier, inc=1, device_id=(dp + 1 - 2 * core, y), device_id_type=MESH)
 
-        def greet(step, carry):
-            column = (x + step) % 4
-            for n in range(15):
-                peer = column * 16 + (z + 8 + around(n)) % 16
-                pl.semaphore_signal(barrier, inc=1, device_id=(peer * 2 + core, y), device_id_type=MESH)
-
-            @pl.when(column != x)
-            def _():
-                pl.semaphore_signal(barrier, inc=1, device_id=((column * 16 + z) * 2 + core, y), device_id_type=MESH)
-
-            return carry
-
-        lax.fori_loop(1, 5, greet, 0)
+        for n in range(16):
+            for h in (2, 1, 3, 0):
+                if n < 15 or h:
+                    peer = (x + h) % 4 * 16 + (z + 8 + around(n)) % 16
+                    pl.semaphore_signal(barrier, inc=1, device_id=(peer * 2 + core, y), device_id_type=MESH)
 
     @pl.when(jnp.logical_not(works))
     def _():
@@ -136,7 +128,7 @@
     own = pltpu.make_async_copy(staged.at[y], from_y.at[y], local_y)
     own.start()
     for i in range(3):
-        for step in range(1, N_TENSOR):
+        for step in (2, 1, 3):
             y_copy(staged, from_y, step, i, send_y, recv_y).start()
     own.wait()
 
@@ -283,7 +275,7 @@
         pltpu.make_async_copy(four, four, recv_b.at[t]).wait()
         tile = back[pl.ds(4 * t, 4)].reshape(4 * BAND, WIDE)
         to_y[:, at, :] = permuted(regroup, tile).reshape(4, BAND, WIDE)
-        for step in range(1, N_TENSOR):
+        for step in (2, 1, 3):
             y_copy(to_y, land, step, i, send_z, recv_z).start()
 
     own = pltpu.make_async_copy(to_y.at[y], land.at[y], local_z)

time: 80.7 us -> 80 us (level)
  no operation moved by 1% of the time
where the time goes in v8:
time: 80 us; the launch traced here: 79.8 us
  Pallas kernels  77.2 us (96%)
  local copies, waits for them, and re-layouts  2.02 us (3%)
    pallas_call x1, Pallas kernels, on_device(): pl.pallas_call(kernel, out_shape=(jax.ShapeDtypeStruct(momentum.shape, f3...  77.2 us
    unnamed x3, local copies, waits for them, and re-layouts  2.02 us

profile of v8, /device:TPU:1, one launch (start us, length us, event | category | flops | bytes accessed | tf_op | source)
XLA Modules:
  0.0 79.8 jit_solution(16594191500929152136)
XLA Ops:
  0.6 77.2 %shard_map.58 = (f32[48,2816]{1,0:T(8,128)S(1)}, bf16[48,2816]{1,0:T(8,128)(2,1)S(1)}, f32[1,2]{1,0:T(1,128)S(1)}) custom-call(bf16[48,2816]{1,0:T(8,128)(2,1)} %grad_ref.1, f32[48,2816]{1,0:T(8,128)} %momentum_ref.1, s32[1,48]{1,0:T(1,128)} %bitcast.1), custom_call_target="tpu_custom_call" | custom-call | tf_op jit(solution)/shard_map/pallas_call | solution.py:323
  77.8 0.8 %copy.9 = f32[48,2816]{1,0:T(8,128)} copy(f32[48,2816]{1,0:T(8,128)S(1)} %get-tuple-element.6) | data formatting | bytes 1081344
  78.6 0.7 copy.10
  79.3 0.5 copy.11

commit v9 on v8

--- a/solution.py
+++ b/solution.py
@@ -125,11 +125,11 @@
             device_id=(dp, peer), device_id_type=MESH,
         )
 
-    own = pltpu.make_async_copy(staged.at[y], from_y.at[y], local_y)
-    own.start()
     for i in range(3):
         for step in (2, 1, 3):
             y_copy(staged, from_y, step, i, send_y, recv_y).start()
+    own = pltpu.make_async_copy(staged.at[y], from_y.at[y], local_y)
+    own.start()
     own.wait()
 
     def band_copy(i, k):
@@ -179,19 +179,17 @@
             half[turn, c, upper(c)[0]] = value.astype(bf16)
             swap(turn, c).start()
 
-        def gram_sum(turn):
-            for c in (2, 1, 0):
-                swap(turn, c).wait()
-                over, across = upper(c)
-                total[over, across] = half[turn, c, over].astype(f32) + other[turn, c, over].astype(f32)
-
-        def set_gram(scale):
-            for c in range(WIDE // TILE):
-                over, across = upper(c)
-                block = (total[over, across] * scale * scale).astype(bf16)
-                gram[over, across] = block
-                for r in range(c):
-                    gram[across, r * TILE:(r + 1) * TILE] = block[r * TILE:(r + 1) * TILE].T
+        def whole(turn, c):
+            swap(turn, c).wait()
+            over = upper(c)[0]
+            return half[turn, c, over].astype(f32) + other[turn, c, over].astype(f32)
+
+        def set_gram(c, value):
+            over, across = upper(c)
+            block = value.astype(bf16)
+            gram[over, across] = block
+            for r in range(c):
+                gram[across, r * TILE:(r + 1) * TILE] = block[r * TILE:(r + 1) * TILE].T
 
         def polynomial():
             current = gram[...]
@@ -216,14 +214,16 @@
                 else:
                     total[over, across] = value
 
-        gram_sum(0)
+        for c in (2, 1, 0):
+            total[upper(c)] = whole(0, c)
         diagonal = lax.broadcasted_iota(jnp.int32, (TILE, TILE), 0) == lax.broadcasted_iota(jnp.int32, (TILE, TILE), 1)
         on_diagonal = sum(
             jnp.where(diagonal, total[c * TILE:(c + 1) * TILE, c * TILE:(c + 1) * TILE], 0.0) for c in range(WIDE // TILE)
         )
         squares = jnp.sum(jnp.sum(on_diagonal, axis=1, keepdims=True), axis=0, keepdims=True)
         inverse = 1.0 / (jnp.sqrt(squares) + epsilon)
-        set_gram(inverse)
+        for c in range(WIDE // TILE):
+            set_gram(c, total[upper(c)] * inverse * inverse)
         polynomial()
 
         for b in range(ROWS // TILE):
@@ -238,8 +238,8 @@
             over, across = upper(c)
             right = mid[:, :, across].reshape(ROWS, TILE)
             give_half(1, c, jnp.dot(turned[over], right, preferred_element_type=f32))
-        gram_sum(1)
-        set_gram(1.0)
+        for c in (2, 1, 0):
+            set_gram(c, whole(1, c))
         polynomial()
 
         rms = jnp.sqrt(squares / (D * HW))

time: 80 us -> 79.9 us (level)
  no operation moved by 1% of the time
where the time goes in v9:
time: 79.9 us; the launch traced here: 79.7 us
  Pallas kernels  77.1 us (96%)
  local copies, waits for them, and re-layouts  2.02 us (3%)
    pallas_call x1, Pallas kernels, on_device(): pl.pallas_call(kernel, out_shape=(jax.ShapeDtypeStruct(momentum.shape, f3...  77.1 us
    unnamed x3, local copies, waits for them, and re-layouts  2.02 us

profile of v9, /device:TPU:1, one launch (start us, length us, event | category | flops | bytes accessed | tf_op | source)
XLA Modules:
  0.0 79.7 jit_solution(12689358705308305841)
XLA Ops:
  0.6 77.1 %shard_map.58 = (f32[48,2816]{1,0:T(8,128)S(1)}, bf16[48,2816]{1,0:T(8,128)(2,1)S(1)}, f32[1,2]{1,0:T(1,128)S(1)}) custom-call(bf16[48,2816]{1,0:T(8,128)(2,1)} %grad_ref.1, f32[48,2816]{1,0:T(8,128)} %momentum_ref.1, s32[1,48]{1,0:T(1,128)} %bitcast.1), custom_call_target="tpu_custom_call" | custom-call | tf_op jit(solution)/shard_map/pallas_call | solution.py:323
  77.7 0.8 %copy.9 = f32[48,2816]{1,0:T(8,128)} copy(f32[48,2816]{1,0:T(8,128)S(1)} %get-tuple-element.6) | data formatting | bytes 1081344
  78.5 0.7 copy.10
  79.2 0.5 copy.11

commit v10 on v9

--- a/solution.py
+++ b/solution.py
@@ -265,7 +265,12 @@
             for n, (d, r) in enumerate(peers):
                 for h in (2, 1, 3, 0):
                     if d or n < 3 or h:
-                        give((x + h) % 4, quarter(d) * 4 + r).start()
+                        if len(ds) == 2:
+                            side = 1 + 2 * ((n + core) % 2)
+                            at_z = quarter(side) * 4 + jnp.where(side == 1, 3 - n // 2, n // 2)
+                        else:
+                            at_z = quarter(d) * 4 + r
+                        give((x + 4 + h * (1 - 2 * core)) % 4, at_z).start()
 
         pltpu.make_async_copy(done.at[slot], back.at[mine], recv_b.at[mine // 4]).start()
 

time: 79.9 us -> 80.7 us (1.010)
    pallas_call x1, Pallas kernels: 77.1 us -> 77.9 us  [on_device(): pl.pallas_call(kernel, out_shape=(jax.ShapeDtypeStruct(momentum.shape, f3...]
where the time goes in v10:
time: 80.7 us; the launch traced here: 80.6 us
  Pallas kernels  77.9 us (97%)
  local copies, waits for them, and re-layouts  2.02 us (3%)
    pallas_call x1, Pallas kernels, on_device(): pl.pallas_call(kernel, out_shape=(jax.ShapeDtypeStruct(momentum.shape, f3...  77.9 us
    unnamed x3, local copies, waits for them, and re-layouts  2.02 us

profile of v10, /device:TPU:1, one launch (start us, length us, event | category | flops | bytes accessed | tf_op | source)
XLA Modules:
  0.0 80.6 jit_solution(6656187830073832539)
XLA Ops:
  0.6 77.9 %shard_map.58 = (f32[48,2816]{1,0:T(8,128)S(1)}, bf16[48,2816]{1,0:T(8,128)(2,1)S(1)}, f32[1,2]{1,0:T(1,128)S(1)}) custom-call(bf16[48,2816]{1,0:T(8,128)(2,1)} %grad_ref.1, f32[48,2816]{1,0:T(8,128)} %momentum_ref.1, s32[1,48]{1,0:T(1,128)} %bitcast.1), custom_call_target="tpu_custom_call" | custom-call | tf_op jit(solution)/shard_map/pallas_call | solution.py:328
  78.6 0.8 copy.9
  79.4 0.7 copy.10
  80.1 0.5 copy.11
